TPU v7x, 32 devices: a whole 2x2x4 slice. The times are simulated.
32 devices in a mesh: dp: 16 (over z, y, x), frame: 2 (over core).
Axes of the slice: x: 2, y: 2, z: 4, core: 2. Of those that a mesh axis runs over, the one named last changes fastest.
Arguments:
- tokens: bfloat16 [2, 16, 2, 256, 1024], P(None, 'dp', 'frame'), may hold values from -6 to 6
- memory: bfloat16 [2, 16, 2, 256, 1024], P(None, 'dp', None, 'frame'), may hold values from -6 to 6
- token_lengths: int32 [2, 16, 2, 4], P(None, 'dp'), may hold values from 1 to 128, 256 in all within a row
- frame_lengths: int32 [2, 16, 2, 4], P(None, 'dp'), may hold values from 1 to 192, 256 in all within a row
- attention_in: bfloat16 [2, 3, 1024, 1024], replicated, may hold values from -0.1875 to 0.1875
- attention_out: bfloat16 [2, 1024, 1024], replicated, may hold values from -0.75 to 0.75
- attention_bias: float32 [2, 3, 1024], replicated, may hold values from -1.5 to 1.5
- norm_gain: float32 [4, 1024], replicated, may hold values from 0.25 to 1.75
- norm_bias: float32 [4, 1024], replicated, may hold values from -1.5 to 1.5
- expand_weight: bfloat16 [1024, 4096], replicated, may hold values from -0.1875 to 0.1875
- expand_bias: float32 [4096], replicated, may hold values from -1.5 to 1.5
- reduce_weight: bfloat16 [4096, 1024], replicated, may hold values from -0.1875 to 0.1875
- reduce_bias: float32 [1024], replicated, may hold values from -1.5 to 1.5
- cotangent: bfloat16 [2, 16, 2, 256, 1024], P(None, 'dp', 'frame'), may hold values from -6 to 6
Outputs:
- out_tokens: bfloat16 [2, 16, 2, 256, 1024], P(None, 'dp', 'frame')
- grad_tokens: float32 [2, 16, 2, 256, 1024], P(None, 'dp', 'frame')
- grad_memory: float32 [2, 16, 2, 256, 1024], P(None, 'dp', None, 'frame')
- grad_attention_in: float32 [2, 3, 1024, 1024], P(None, None, ('dp', 'frame'))
- grad_attention_out: float32 [2, 1024, 1024], P(None, ('dp', 'frame'))
- grad_attention_bias: float32 [2, 3, 1024], P(None, None, ('dp', 'frame'))
- grad_norm_gain: float32 [4, 1024], P(None, ('dp', 'frame'))
- grad_norm_bias: float32 [4, 1024], P(None, ('dp', 'frame'))
- grad_expand_weight: float32 [1024, 4096], P(('dp', 'frame'))
- grad_expand_bias: float32 [4096], P(('dp', 'frame'))
- grad_reduce_weight: float32 [4096, 1024], P(('dp', 'frame'))
- grad_reduce_bias: float32 [1024], P(('dp', 'frame'))
Inputs may be any that keep to these rules, and one draw needn't show every extreme that they name: `token_lengths`: each list of 4 lengths sums to 256, and its longest is 128. `frame_lengths`: each list of 4 lengths sums to 256, and its longest is 192.
All inputs are finite; a program needn't handle non-finite values.
Results may differ from a plain program's by a relative error of at most 0.015.
Values may be sent and summed in bfloat16 or wider, within the bound.
A program may use at most 320 MiB of HBM per device.

v0:
```python
import math

import jax
import jax.numpy as jnp
from jax import lax
from jax.sharding import PartitionSpec as P

D = 1024
HEADS = 16
HEAD_DIM = 64


def merged(part, axis, combine):
    gathered = jax.tree.map(lambda a: lax.all_gather(a, axis), part)

    def take(source):
        return jax.tree.map(lambda a: lax.dynamic_index_in_dim(a, source, 0, False), gathered)

    return lax.fori_loop(
        1, lax.axis_size(axis), lambda source, state: combine(state, take(source)), take(0)
    )


def norm_rows(values, gains, shifts):
    centre = jnp.mean(values, axis=-1, keepdims=True)
    offset = values - centre
    spread = jnp.mean(offset * offset, axis=-1, keepdims=True)
    return offset * lax.rsqrt(spread + 1e-05) * gains + shifts


def segment_ids(lengths, count):
    bounds = jnp.cumsum(lengths, axis=-1)
    positions = jnp.arange(count, dtype=jnp.int32)
    return jnp.sum((positions[None, :, None] >= bounds[:, None, :]).astype(jnp.int32), axis=-1)


def split_heads(values):
    return values.reshape(values.shape[:-1] + (HEADS, HEAD_DIM))


def gelu_tanh(values):
    return jax.nn.gelu(values, approximate=True)


def product(left, right):
    return jnp.dot(left, right, preferred_element_type=jnp.float32)


def left_product(left, right):
    return jnp.einsum("rd,re->de", left, right, preferred_element_type=jnp.float32)


def right_product(left, right):
    return jnp.einsum("re,de->rd", left, right, preferred_element_type=jnp.float32)


def column_sum(values):
    return jnp.sum(values.astype(jnp.float32), axis=0)


def merge_softmax(left_part, right_part):
    peak_left, total_left, sums_left = left_part
    peak_right, total_right, sums_right = right_part
    peak = jnp.maximum(peak_left, peak_right)
    scale_left = jnp.exp(peak_left - peak)
    scale_right = jnp.exp(peak_right - peak)
    total = total_left * scale_left + total_right * scale_right
    combined = (
        split_heads(sums_left) * scale_left[..., None]
        + split_heads(sums_right) * scale_right[..., None]
    )
    return (peak, total, combined.reshape(sums_left.shape))


def local(
    tokens,
    memory,
    token_lengths,
    frame_lengths,
    attention_in,
    attention_out,
    attention_bias,
    norm_gain,
    norm_bias,
    expand_weight,
    expand_bias,
    reduce_weight,
    reduce_bias,
    cotangent,
):
    highest = lax.Precision.HIGHEST
    frame_side = lax.axis_index("frame")
    row_count = tokens.shape[3]
    half_frames = memory.shape[3]
    all_frames = half_frames * lax.axis_size("frame")
    factor = 1.0 / math.sqrt(HEAD_DIM)
    positions = jnp.arange(row_count, dtype=jnp.int32)
    causal = positions[None, :] <= positions[:, None]
    grad_attention_in = jnp.zeros(attention_in.shape, jnp.float32)
    grad_attention_out = jnp.zeros(attention_out.shape, jnp.float32)
    grad_attention_bias = jnp.zeros(attention_bias.shape, jnp.float32)
    grad_norm_gain = jnp.zeros(norm_gain.shape, jnp.float32)
    grad_norm_bias = jnp.zeros(norm_bias.shape, jnp.float32)
    grad_expand = jnp.zeros(expand_weight.shape, jnp.float32)
    grad_expand_bias = jnp.zeros(expand_bias.shape, jnp.float32)
    grad_reduce = jnp.zeros(reduce_weight.shape, jnp.float32)
    grad_reduce_bias = jnp.zeros(reduce_bias.shape, jnp.float32)
    output_list = []
    grad_token_list = []
    grad_memory_list = []
    for microbatch in range(tokens.shape[0]):
        hidden = tokens[microbatch, 0, 0].astype(jnp.float32)
        memory_local = memory[microbatch, 0]
        token_seg = segment_ids(token_lengths[microbatch, 0], row_count)
        frame_seg = segment_ids(frame_lengths[microbatch, 0], all_frames)
        own_seg = lax.dynamic_index_in_dim(token_seg, frame_side, 0, keepdims=False)
        self_mask = ((own_seg[:, None] == own_seg[None, :]) & causal)[None]
        normed_self, pull_self = jax.vjp(norm_rows, hidden, norm_gain[0], norm_bias[0])
        input_self = normed_self.astype(jnp.bfloat16)
        query_self = (product(input_self, attention_in[0, 0]) + attention_bias[0, 0]).astype(
            jnp.bfloat16
        )
        key_self = product(input_self, attention_in[0, 1]).astype(jnp.bfloat16)
        value_self = (product(input_self, attention_in[0, 2]) + attention_bias[0, 1]).astype(
            jnp.bfloat16
        )
        scores_self = (
            jnp.einsum(
                "qhd,khd->hqk",
                split_heads(query_self),
                split_heads(key_self),
                preferred_element_type=jnp.float32,
            )
            * factor
        )
        scores_self = jnp.where(self_mask, scores_self, -1e30)
        peak_self = jnp.max(scores_self, axis=-1, keepdims=True)
        weights_self = jnp.exp(scores_self - peak_self)
        total_self = jnp.sum(weights_self, axis=-1, keepdims=True)
        logsum_self = peak_self + jnp.log(total_self)
        context_self = (
            jnp.einsum(
                "hqk,khd->qhd",
                (weights_self / total_self).astype(jnp.bfloat16),
                split_heads(value_self),
                preferred_element_type=jnp.float32,
            )
            .reshape(row_count, D)
            .astype(jnp.bfloat16)
        )
        after_self = hidden + product(context_self, attention_out[0]) + attention_bias[0, 2]
        normed_cross, pull_cross = jax.vjp(norm_rows, after_self, norm_gain[1], norm_bias[1])
        input_cross = normed_cross.astype(jnp.bfloat16)
        query_cross = (product(input_cross, attention_in[1, 0]) + attention_bias[1, 0]).astype(
            jnp.bfloat16
        )
        key_local = jnp.einsum(
            "amd,de->ame", memory_local, attention_in[1, 1], preferred_element_type=jnp.float32
        ).astype(jnp.bfloat16)
        value_local = (
            jnp.einsum(
                "amd,de->ame", memory_local, attention_in[1, 2], preferred_element_type=jnp.float32
            )
            + attention_bias[1, 1]
        ).astype(jnp.bfloat16)
        query_pair = lax.all_gather(query_cross[None], "frame", axis=0, tiled=True)
        local_seg = lax.dynamic_slice_in_dim(frame_seg, frame_side * half_frames, half_frames, 1)
        pair_mask = (token_seg[:, :, None] == local_seg[:, None, :])[:, :, None, :]
        raw_cross = (
            jnp.einsum(
                "aqhd,akhd->aqhk",
                split_heads(query_pair),
                split_heads(key_local),
                preferred_element_type=jnp.float32,
            )
            * factor
        )
        raw_cross = jnp.where(pair_mask, raw_cross, -1e30)
        peak_cross = jnp.max(raw_cross, axis=-1)
        weights_cross = jnp.where(pair_mask, jnp.exp(raw_cross - peak_cross[..., None]), 0.0)
        total_cross = jnp.sum(weights_cross, axis=-1)
        sums_cross = jnp.einsum(
            "aqhk,akhd->aqhd",
            weights_cross,
            split_heads(value_local).astype(jnp.float32),
            precision=highest,
        ).reshape(query_pair.shape)
        peak_all, total_all, sums_all = merged(
            (peak_cross, total_cross, sums_cross), "frame", merge_softmax
        )
        context_pair = split_heads(sums_all) / total_all[..., None]
        logsum_pair = peak_all + jnp.log(total_all)
        context_exact = lax.dynamic_index_in_dim(
            context_pair, frame_side, 0, keepdims=False
        ).reshape(row_count, D)
        context_cross = context_exact.astype(jnp.bfloat16)
        after_cross = after_self + product(context_cross, attention_out[1]) + attention_bias[1, 2]
        normed_ffn, pull_ffn = jax.vjp(norm_rows, after_cross, norm_gain[2], norm_bias[2])
        input_ffn = normed_ffn.astype(jnp.bfloat16)
        pre_act = product(input_ffn, expand_weight) + expand_bias
        act_value, pull_act = jax.vjp(gelu_tanh, pre_act)
        act_low = act_value.astype(jnp.bfloat16)
        after_ffn = after_cross + product(act_low, reduce_weight) + reduce_bias
        final_value, pull_final = jax.vjp(norm_rows, after_ffn, norm_gain[3], norm_bias[3])
        output_list.append(final_value.astype(jnp.bfloat16))
        grad_ffn_res, gain_final, shift_final = pull_final(
            cotangent[microbatch, 0, 0].astype(jnp.float32)
        )
        grad_fed = grad_ffn_res.astype(jnp.bfloat16)
        grad_reduce = grad_reduce + left_product(act_low, grad_fed)
        grad_reduce_bias = grad_reduce_bias + column_sum(grad_fed)
        grad_pre = pull_act(right_product(grad_fed, reduce_weight))[0].astype(jnp.bfloat16)
        grad_expand = grad_expand + left_product(input_ffn, grad_pre)
        grad_expand_bias = grad_expand_bias + column_sum(grad_pre)
        grad_norm_ffn, gain_ffn, shift_ffn = pull_ffn(right_product(grad_pre, expand_weight))
        grad_cross_res = grad_ffn_res + grad_norm_ffn
        grad_crossed = grad_cross_res.astype(jnp.bfloat16)
        grad_out_cross = left_product(context_cross, grad_crossed)
        bias_out_cross = column_sum(grad_crossed)
        grad_context = right_product(grad_crossed, attention_out[1]).astype(jnp.bfloat16)
        grad_pair = lax.all_gather(grad_context[None], "frame", axis=0, tiled=True)
        grad_heads = split_heads(grad_pair)
        spread_cross = jnp.sum(grad_heads.astype(jnp.float32) * context_pair, axis=-1)
        probs_cross = jnp.where(pair_mask, jnp.exp(raw_cross - logsum_pair[..., None]), 0.0)
        grad_probs = jnp.einsum(
            "aqhd,akhd->aqhk",
            grad_heads,
            split_heads(value_local),
            preferred_element_type=jnp.float32,
        )
        grad_scores = (probs_cross * (grad_probs - spread_cross[..., None])).astype(jnp.bfloat16)
        query_part = (
            jnp.einsum(
                "aqhk,akhd->aqhd",
                grad_scores,
                split_heads(key_local),
                preferred_element_type=jnp.float32,
            )
            * factor
        ).reshape(query_pair.shape)
        grad_key_local = (
            (
                jnp.einsum(
                    "aqhk,aqhd->akhd",
                    grad_scores,
                    split_heads(query_pair),
                    preferred_element_type=jnp.float32,
                )
                * factor
            )
            .reshape(key_local.shape)
            .astype(jnp.bfloat16)
        )
        grad_value_local = (
            jnp.einsum(
                "aqhk,aqhd->akhd", probs_cross, grad_heads.astype(jnp.float32), precision=highest
            )
            .reshape(value_local.shape)
            .astype(jnp.bfloat16)
        )
        grad_query = (
            lax.psum_scatter(
                query_part.astype(jnp.bfloat16), "frame", scatter_dimension=0, tiled=True
            )
            .astype(jnp.float32)[0]
            .astype(jnp.bfloat16)
        )
        grad_query_cross = left_product(input_cross, grad_query)
        bias_query_cross = column_sum(grad_query)
        grad_key_cross = jnp.einsum(
            "amd,ame->de", memory_local, grad_key_local, preferred_element_type=jnp.float32
        )
        grad_value_cross = jnp.einsum(
            "amd,ame->de", memory_local, grad_value_local, preferred_element_type=jnp.float32
        )
        bias_value_cross = jnp.sum(grad_value_local.astype(jnp.float32), axis=(0, 1))
        grad_memory_local = jnp.einsum(
            "ame,de->amd", grad_key_local, attention_in[1, 1], preferred_element_type=jnp.float32
        ) + jnp.einsum(
            "ame,de->amd", grad_value_local, attention_in[1, 2], preferred_element_type=jnp.float32
        )
        grad_memory_list.append(grad_memory_local)
        grad_norm_cross, gain_cross, shift_cross = pull_cross(
            right_product(grad_query, attention_in[1, 0])
        )
        grad_self_res = grad_cross_res + grad_norm_cross
        grad_attended = grad_self_res.astype(jnp.bfloat16)
        grad_out_self = left_product(context_self, grad_attended)
        bias_out_self = column_sum(grad_attended)
        grad_context_self = right_product(grad_attended, attention_out[0]).astype(jnp.bfloat16)
        probs_self = jnp.exp(scores_self - logsum_self)
        grad_probs_self = jnp.einsum(
            "qhd,khd->hqk",
            split_heads(grad_context_self),
            split_heads(value_self),
            preferred_element_type=jnp.float32,
        )
        spread_self = jnp.sum(grad_probs_self * probs_self, axis=-1, keepdims=True)
        grad_scores_self = (probs_self * (grad_probs_self - spread_self)).astype(jnp.bfloat16)
        grad_query_self = (
            (
                jnp.einsum(
                    "hqk,khd->qhd",
                    grad_scores_self,
                    split_heads(key_self),
                    preferred_element_type=jnp.float32,
                )
                * factor
            )
            .reshape(row_count, D)
            .astype(jnp.bfloat16)
        )
        grad_key_self = (
            (
                jnp.einsum(
                    "hqk,qhd->khd",
                    grad_scores_self,
                    split_heads(query_self),
                    preferred_element_type=jnp.float32,
                )
                * factor
            )
            .reshape(row_count, D)
            .astype(jnp.bfloat16)
        )
        grad_value_self = (
            jnp.einsum(
                "hqk,qhd->khd",
                probs_self.astype(jnp.bfloat16),
                split_heads(grad_context_self),
                preferred_element_type=jnp.float32,
            )
            .reshape(row_count, D)
            .astype(jnp.bfloat16)
        )
        grad_input_self = (
            right_product(grad_query_self, attention_in[0, 0])
            + right_product(grad_key_self, attention_in[0, 1])
            + right_product(grad_value_self, attention_in[0, 2])
        )
        grad_hidden, gain_self, shift_self = pull_self(grad_input_self)
        grad_token_list.append(grad_self_res + grad_hidden)
        grad_attention_in = grad_attention_in + jnp.stack(
            [
                jnp.stack(
                    [
                        left_product(input_self, grad_query_self),
                        left_product(input_self, grad_key_self),
                        left_product(input_self, grad_value_self),
                    ]
                ),
                jnp.stack([grad_query_cross, grad_key_cross, grad_value_cross]),
            ]
        )
        grad_attention_out = grad_attention_out + jnp.stack([grad_out_self, grad_out_cross])
        grad_attention_bias = grad_attention_bias + jnp.stack(
            [
                jnp.stack(
                    [column_sum(grad_query_self), column_sum(grad_value_self), bias_out_self]
                ),
                jnp.stack([bias_query_cross, bias_value_cross, bias_out_cross]),
            ]
        )
        grad_norm_gain = grad_norm_gain + jnp.stack([gain_self, gain_cross, gain_ffn, gain_final])
        grad_norm_bias = grad_norm_bias + jnp.stack(
            [shift_self, shift_cross, shift_ffn, shift_final]
        )
    summed = (
        lax.psum_scatter(grad_attention_in, ("dp", "frame"), scatter_dimension=2, tiled=True),
        lax.psum_scatter(grad_attention_out, ("dp", "frame"), scatter_dimension=1, tiled=True),
        lax.psum_scatter(grad_attention_bias, ("dp", "frame"), scatter_dimension=2, tiled=True),
        lax.psum_scatter(grad_norm_gain, ("dp", "frame"), scatter_dimension=1, tiled=True),
        lax.psum_scatter(grad_norm_bias, ("dp", "frame"), scatter_dimension=1, tiled=True),
        lax.psum_scatter(grad_expand, ("dp", "frame"), scatter_dimension=0, tiled=True),
        lax.psum_scatter(grad_expand_bias, ("dp", "frame"), scatter_dimension=0, tiled=True),
        lax.psum_scatter(grad_reduce, ("dp", "frame"), scatter_dimension=0, tiled=True),
        lax.psum_scatter(grad_reduce_bias, ("dp", "frame"), scatter_dimension=0, tiled=True),
    )
    out_tokens = jnp.stack(output_list)[:, None, None]
    grad_tokens = jnp.stack(grad_token_list)[:, None, None]
    grad_memory = jnp.stack(grad_memory_list)[:, None]
    return (
        out_tokens,
        grad_tokens,
        grad_memory,
        summed[0],
        summed[1],
        summed[2],
        summed[3],
        summed[4],
        summed[5],
        summed[6],
        summed[7],
        summed[8],
    )


def solution(mesh):
    placed = (
        P(None, "dp", "frame", None, None),
        P(None, "dp", None, "frame", None),
        P(None, "dp", None, None),
        P(None, "dp", None, None),
        P(),
        P(),
        P(),
        P(),
        P(),
        P(),
        P(),
        P(),
        P(),
        P(None, "dp", "frame", None, None),
    )
    return jax.shard_map(
        local,
        mesh=mesh,
        in_specs=placed,
        out_specs=(
            P(None, "dp", "frame", None, None),
            P(None, "dp", "frame", None, None),
            P(None, "dp", None, "frame", None),
            P(None, None, ("dp", "frame"), None),
            P(None, ("dp", "frame"), None),
            P(None, None, ("dp", "frame")),
            P(None, ("dp", "frame")),
            P(None, ("dp", "frame")),
            P(("dp", "frame"), None),
            P(("dp", "frame")),
            P(("dp", "frame"), None),
            P(("dp", "frame")),
        ),
        check_vma=False,
    )
```

profile of v0, /device:TPU:0, one launch (start us, length us, event | category | flops | bytes accessed | tf_op | source)
XLA Modules:
  0.0 1492.6 jit_solution(7320975612229506650)
XLA Ops:
  109.0 4.9 fusion.413
  124.7 6.0 convolution_add_fusion.2
  150.6 6.5 convolution_add_fusion.3
  164.6 7.9 convert_reduce_fusion
  173.5 8.1 convert_reduce_fusion.1
  181.6 6.5 fusion.425
  188.2 7.1 multiply_reduce_fusion.4
  207.0 5.0 all-gather.23.cloned.1.call-done
  261.6 6.6 convert_reduce_fusion.15
  326.1 9.3 maximum_add_fusion.1
  340.0 10.1 convolution_add_fusion.1
  351.1 10.9 fusion.387
  362.1 11.1 convolution_add_fusion
  404.5 5.3 maximum_bitcast_fusion.3
  409.8 10.7 maximum_bitcast_fusion
  420.5 6.6 maximum_bitcast_fusion.1
  427.1 18.8 %maximum_add_fusion = f32[2,3,1024,1024]{3,2,1,0:T(8,128)} fusion(f32[1,3,1024,1024]{3,2,1,0:T(8,128)} %maximum_bitcast_fusion.1, f32[1,3,1024,1024]{3,2,1,0:T(8,128)} %maximum_bitcast_fusion, f32[1,3,1024,1024]{3,2,1,0:T(8,128)S(1)} %maximum_bitcast_fusion.3, f32[1,3,1024,1024]{3,2,1,0:T(8,128)S(1)} %maximum_bitcast_fusion.2), kind=kLoop, calls=%fused_computation | loop fusion | flops 18874368 | bytes 75497472 | tf_op jit(solution)/shard_map/add | solution.py:343
  446.6 40.6 %all-reduce.2 = (f32[4096]{0:T(1024)S(1)}, f32[1024]{0:T(1024)S(1)}) all-reduce(f32[4096]{0:T(1024)S(1)} %add.587, f32[1024]{0:T(1024)S(1)} %add.589), channel_id=18, replica_groups=mesh['dp'=16,'frame'=2] {'dp','frame'}, use_global_device_ids=true, to_apply=%region_90.91.clone | all-reduce | flops 5120 | bytes 40960
  505.0 78.2 %reduce-scatter.30.cloned.1.call-done = f32[32,4]{1,0:T(8,128)} async-done(((f32[1024,4]{1,0:T(8,128)}), f32[32,4]{1,0:T(8,128)}) %reduce-scatter.30.cloned.1.call-update) | async-done | bytes 528
  584.5 130.9 %reduce-scatter.28.cloned.1.call-done = f32[32,6]{1,0:T(8,128)} async-done(((f32[1024,6]{1,0:T(8,128)}), f32[32,6]{1,0:T(8,128)}) %reduce-scatter.28.cloned.1.call-update) | async-done | bytes 784
  716.8 146.2 %reduce-scatter.22.cloned.1.call-done = f32[2,32,1024]{2,1,0:T(8,128)} async-done(((f32[2,1024,1024]{2,1,0:T(8,128)}), f32[2,32,1024]{2,1,0:T(8,128)}) %reduce-scatter.22.cloned.1.call-update) | async-done | bytes 262160 | tf_op jit(solution)/shard_map/reduce_scatter | solution.py:370
  863.1 181.7 %reduce-scatter.24.cloned.1.call-done = f32[32,4096]{1,0:T(8,128)} async-done(((f32[1024,4096]{1,0:T(8,128)}), f32[32,4096]{1,0:T(8,128)}) %reduce-scatter.24.cloned.1.call-update) | async-done | bytes 524304 | tf_op jit(solution)/shard_map/reduce_scatter | solution.py:374
  1044.7 187.4 %reduce-scatter.26.cloned.1.call-done = f32[128,1024]{1,0:T(8,128)} async-done(((f32[4096,1024]{1,0:T(8,128)}), f32[128,1024]{1,0:T(8,128)}) %reduce-scatter.26.cloned.1.call-update) | async-done | bytes 524304 | tf_op jit(solution)/shard_map/reduce_scatter | solution.py:376
  1232.2 253.4 %reduce-scatter.20.cloned.1.call-done = f32[2,3,32,1024]{3,2,1,0:T(8,128)} async-done(((f32[2,3,1024,1024]{3,2,1,0:T(8,128)}), f32[2,3,32,1024]{3,2,1,0:T(8,128)}) %reduce-scatter.20.cloned.1.call-update) | async-done | bytes 786448 | tf_op jit(solution)/shard_map/reduce_scatter | solution.py:369
  (707 shorter events, 315.1 us)
Async XLA Ops:
  7.2 51.4 %all-gather.21.cloned.1.call-start = ((), (), s32[]{:S(2)}) async-start(), calls=%async_computation.18 | async-start | bytes 1572864 | tf_op jit(solution)/shard_map/all_gather | solution.py:166
  33.1 48.8 %all-gather.19.cloned.1.call-start = ((), (), s32[]{:S(2)}) async-start(), calls=%async_computation.17 | async-start | bytes 1572864 | tf_op jit(solution)/shard_map/all_gather | solution.py:166
  51.2 57.8 %all-gather.17.cloned.1.call-start = ((), (), s32[]{:S(2)}) async-start(), calls=%async_computation.10 | async-start | bytes 6291456 | tf_op jit(solution)/shard_map/all_gather | solution.py:14
  58.6 40.7 %copy-start.111 = (pred[2,256,128]{1,2,0:T(8,128)(4,1)}, pred[2,256,128]{1,2,0:T(8,128)(4,1)S(1)}, u32[]{:S(2)}) copy-start(pred[2,256,128]{1,2,0:T(8,128)(4,1)S(1)} %broadcast_compare_fusion) | copy-start | bytes 196612
  74.4 60.5 %all-gather.15.cloned.1.call-start = ((), (), s32[]{:S(2)}) async-start(), calls=%async_computation.9 | async-start | bytes 6291456 | tf_op jit(solution)/shard_map/all_gather | solution.py:14
  108.7 103.3 %all-gather.23.cloned.1.call-start = ((), (), s32[]{:S(2)}) async-start(), calls=%async_computation.19 | async-start | bytes 1572864 | tf_op jit(solution)/shard_map/all_gather | solution.py:221
  124.4 71.0 %copy-start.154 = (f32[256]{0:T(256)}, f32[256]{0:T(256)S(1)}, u32[]{:S(2)}) copy-start(f32[256]{0:T(256)S(1)} %broadcast_multiply_fusion.1) | copy-start | bytes 3076
  124.6 70.7 %copy-start.171 = (f32[256]{0:T(256)}, f32[256]{0:T(256)S(1)}, u32[]{:S(2)}) copy-start(f32[256]{0:T(256)S(1)} %fusion.366) | copy-start | bytes 3076
  150.3 45.1 %copy-start.6 = (f32[256,1024]{1,0:T(8,128)}, f32[256,1024]{1,0:T(8,128)S(1)}, u32[]{:S(2)}) copy-start(f32[256,1024]{1,0:T(8,128)S(1)} %get-tuple-element.226) | copy-start | bytes 3145732
  150.3 45.1 %copy-start.147 = (f32[256]{0:T(256)}, f32[256]{0:T(256)S(1)}, u32[]{:S(2)}) copy-start(f32[256]{0:T(256)S(1)} %broadcast_multiply_fusion.5) | copy-start | bytes 3076
  150.6 44.8 %copy-start.155 = (f32[256]{0:T(256)}, f32[256]{0:T(256)S(1)}, u32[]{:S(2)}) copy-start(f32[256]{0:T(256)S(1)} %fusion.362) | copy-start | bytes 3076
  200.3 30.9 %all-gather.25.cloned.1.call-start = ((), (), s32[]{:S(2)}) async-start(), calls=%async_computation.20 | async-start | bytes 1572864 | tf_op jit(solution)/shard_map/all_gather | solution.py:221
  207.0 61.8 %reduce-scatter.16.cloned.1.call-start = ((), (), s32[]{:S(2)}) async-start(), calls=%async_computation.11 | async-start | bytes 1572864 | tf_op jit(solution)/shard_map/reduce_scatter | solution.py:262
  229.2 43.1 %reduce-scatter.18.cloned.1.call-start = ((), (), s32[]{:S(2)}) async-start(), calls=%async_computation.12 | async-start | bytes 1572864 | tf_op jit(solution)/shard_map/reduce_scatter | solution.py:262
  248.4 255.2 %reduce-scatter.32.cloned.1.call-start = ((), (), s32[]{:S(2)}) async-start(), calls=%async_computation.23 | async-start | bytes 540672
  315.6 267.5 %reduce-scatter.30.cloned.1.call-start = ((), (), s32[]{:S(2)}) async-start(), calls=%async_computation.22 | async-start | bytes 540672
  320.4 394.9 %reduce-scatter.28.cloned.1.call-start = ((), (), s32[]{:S(2)}) async-start(), calls=%async_computation.21 | async-start | bytes 540672
  326.1 537.0 %reduce-scatter.22.cloned.1.call-start = ((), (), s32[]{:S(2)}) async-start(), calls=%async_computation.14 | async-start | bytes 8650752 | tf_op jit(solution)/shard_map/reduce_scatter | solution.py:370
  335.5 709.2 %reduce-scatter.24.cloned.1.call-start = ((), (), s32[]{:S(2)}) async-start(), calls=%async_computation.15 | async-start | bytes 17301504 | tf_op jit(solution)/shard_map/reduce_scatter | solution.py:374
  350.1 882.1 %reduce-scatter.26.cloned.1.call-start = ((), (), s32[]{:S(2)}) async-start(), calls=%async_computation.16 | async-start | bytes 17301504 | tf_op jit(solution)/shard_map/reduce_scatter | solution.py:376
  373.2 1112.4 %reduce-scatter.20.cloned.1.call-start = ((), (), s32[]{:S(2)}) async-start(), calls=%async_computation.13 | async-start | bytes 25952256 | tf_op jit(solution)/shard_map/reduce_scatter | solution.py:369
  445.9 42.5 %copy-start.90 = (bf16[1,256,1024]{2,1,0:T(8,128)(2,1)S(1)}, bf16[1,256,1024]{2,1,0:T(8,128)(2,1)}, u32[]{:S(2)}) copy-start(bf16[1,256,1024]{2,1,0:T(8,128)(2,1)} %get-tuple-element.185) | copy-start | bytes 1572868
  445.9 42.5 %copy-start.91 = (bf16[1,256,1024]{2,1,0:T(8,128)(2,1)S(1)}, bf16[1,256,1024]{2,1,0:T(8,128)(2,1)}, u32[]{:S(2)}) copy-start(bf16[1,256,1024]{2,1,0:T(8,128)(2,1)} %get-tuple-element.186) | copy-start | bytes 1572868
  445.9 43.6 %copy-start.80 = (bf16[2,16,64,128]{3,2,1,0:T(8,128)(2,1)S(1)}, bf16[2,16,64,128]{3,2,1,0:T(8,128)(2,1)}, u32[]{:S(2)}) copy-start(bf16[2,16,64,128]{3,2,1,0:T(8,128)(2,1)} %copy-done.79) | copy-start | bytes 1572868
  (212 other events, 1166.3 us)
Sparse Core Ops, SparseCore 0:
  33.3 11.7 all-gather.20
  51.3 11.5 all-gather.18
  74.5 16.2 all-gather.16
  108.8 16.0 all-gather.14
  200.5 11.5 all-gather.22
  213.4 10.1 all-gather.24
  229.4 9.6 reduce-scatter.15
  248.5 9.6 reduce-scatter.17
  315.7 135.0 reduce-scatter.31
  453.1 130.0 reduce-scatter.29
  585.4 129.9 reduce-scatter.27
  718.2 144.8 reduce-scatter.21
  866.0 178.6 reduce-scatter.23
  1047.6 184.5 reduce-scatter.25
  1240.2 245.3 reduce-scatter.19
where the time goes:
time: 1500 us; the launch traced here: 1490 us
  waiting for transfers between devices  983 us (66%)
  matrix products  240 us (16%)
  other arithmetic  103 us (7%)
  local copies, waits for them, and re-layouts  97.9 us (7%)
  blocking collectives  48.3 us (3%)
  between operations  17.5 us (1%)
    reduce_scatter x1, waiting for transfers between devices, local(): lax.psum_scatter(grad_attention_in, ('dp', 'frame'), scatter_dimension=2,...  253 us
    unnamed x18, waiting for transfers between devices  209 us
    reduce_scatter x1, waiting for transfers between devices, local(): lax.psum_scatter(grad_reduce, ('dp', 'frame'), scatter_dimension=0, tiled...  187 us
    reduce_scatter x1, waiting for transfers between devices, local(): lax.psum_scatter(grad_expand, ('dp', 'frame'), scatter_dimension=0, tiled...  182 us
    reduce_scatter x1, waiting for transfers between devices, local(): lax.psum_scatter(grad_attention_out, ('dp', 'frame'), scatter_dimension=1...  146 us
    dot_general x16, matrix products, left_product(): jnp.einsum('rd,re->de', left, right, preferred_element_type=jnp.float32)  67.2 us
    dot_general x16, matrix products, right_product(): jnp.einsum('re,de->rd', left, right, preferred_element_type=jnp.float32)  49.9 us
    dot_general x16, matrix products, product(): return jnp.dot(left, right, preferred_element_type=jnp.float32)  42.1 us
  transfers between devices with their start and end apart: 15, of which 7 were waited for; matrix products, arithmetic and copies ran while one was open for 20% of the time, Pallas kernels for 0%

commit v1 on v0

v1 whole, which is shorter than its diff:
```python
import functools
import math

import jax
import jax.numpy as jnp
import numpy as np
from jax import lax
from jax.experimental import pallas as pl
from jax.experimental.pallas import tpu as pltpu
from jax.sharding import PartitionSpec as P

D = 1024
HEADS = 16
HEAD_DIM = 64
FACTOR = 1.0 / math.sqrt(HEAD_DIM)
BF = jnp.bfloat16
F32 = jnp.float32


def dot(a, b):
    return jnp.dot(a, b, preferred_element_type=F32)


def dot_t(a, b):
    return lax.dot_general(a, b, (((1,), (1,)), ((), ())), preferred_element_type=F32)


def norm_stats(v):
    centre = jnp.mean(v, axis=-1, keepdims=True)
    off = v - centre
    r = lax.rsqrt(jnp.mean(off * off, axis=-1, keepdims=True) + 1e-5)
    return off * r, r


def norm_back(e, n, r, gain):
    eg = e * gain
    return r * (
        eg - jnp.mean(eg, axis=-1, keepdims=True) - n * jnp.mean(eg * n, axis=-1, keepdims=True)
    )


def segment_ids(lengths, count):
    bounds = jnp.cumsum(lengths, axis=-1)
    positions = jnp.arange(count, dtype=jnp.int32)
    return jnp.sum((positions[None, :, None] >= bounds[:, None, :]).astype(jnp.int32), axis=-1)


def heads(x, nb):
    return x.reshape(nb, -1, HEADS, HEAD_DIM)


def stage_bits(n_dp):
    m = n_dp.bit_length() - 1
    if m == 4:
        return [[0, 2, 1, 3], [1, 2, 0, 3]]
    evens = [b for b in range(m) if b % 2 == 0]
    odds = [b for b in range(m) if b % 2 == 1]
    one = evens + odds
    two = evens[1:] + evens[:1] + odds[1:] + odds[:1]
    return [one, two]


def place_table(n_dp):
    bits = stage_bits(n_dp)
    n = 2 * n_dp
    m = len(bits[0])
    table = np.zeros((2, n), np.int32)
    for f in range(2):
        for p in range(n):
            far = p >> m
            order = bits[1 - f] if far else bits[f]
            mask = far
            for s in range(m):
                if (p >> (m - 1 - s)) & 1:
                    mask ^= 2 << order[s]
            table[f, p] = mask
    return table


def core_pairs(n_dp):
    return [(d * 2 + f, d * 2 + 1 - f) for d in range(n_dp) for f in range(2)]


def stage_pairs(n_dp, s):
    bits = stage_bits(n_dp)
    return [(d * 2 + f, (d ^ (1 << bits[f][s])) * 2 + f) for d in range(n_dp) for f in range(2)]


AXES = ("dp", "frame")


def permute(x, pairs):
    return lax.ppermute(x, AXES, pairs)


def grad_kernel(half, n_half, r, with_add, table_ref, at_ref, b_ref, *rest):
    if with_add:
        add_ref, send_ref, keep_ref, perm = rest
    else:
        send_ref, perm = rest

    @pl.when(pl.program_id(0) == 0)
    def _():
        for p in range(n_half):
            src = table_ref[half * n_half + p]
            perm[pl.ds(p * r, r), :] = at_ref[pl.ds(pl.multiple_of(src * r, r), r), :]

    rows = n_half * r
    step = min(rows, 512)
    for i in range(rows // step):
        out = dot(perm[pl.ds(i * step, step), :], b_ref[...])
        if not with_add:
            send_ref[pl.ds(i * step, step), :] = out.astype(BF)
        else:
            out = (out + add_ref[pl.ds(i * step, step), :].astype(F32)).astype(BF)
            edge = rows // 2
            lo, hi = i * step, (i + 1) * step
            if lo < edge:
                cut = min(hi, edge)
                keep_ref[pl.ds(lo, cut - lo), :] = out[: cut - lo]
            if hi > edge:
                start = max(lo, edge)
                send_ref[pl.ds(start - edge, hi - start), :] = out[start - lo :]


def grad_half(table, at, b, n, half, add=None):
    feats, rows = at.shape
    cols = b.shape[1]
    r = feats // n
    n_half = n // 2
    tile = min(cols, 512)
    m = n_half * r
    with_add = add is not None
    col = lambda i, t: (0, i)
    in_specs = [pl.BlockSpec((feats, rows), lambda i, t: (0, 0)), pl.BlockSpec((rows, tile), col)]
    args = [at, b]
    if with_add:
        in_specs.append(pl.BlockSpec((m, tile), col))
        args.append(add)
        out_shape = [jax.ShapeDtypeStruct((m // 2, cols), BF)] * 2
        out_specs = [pl.BlockSpec((m // 2, tile), col)] * 2
    else:
        out_shape = jax.ShapeDtypeStruct((m, cols), BF)
        out_specs = pl.BlockSpec((m, tile), col)
    return pl.pallas_call(
        functools.partial(grad_kernel, half, n_half, r, with_add),
        out_shape=out_shape,
        grid_spec=pltpu.PrefetchScalarGridSpec(
            num_scalar_prefetch=1,
            grid=(cols // tile,),
            in_specs=in_specs,
            out_specs=out_specs,
            scratch_shapes=[pltpu.VMEM((m, rows), BF)],
        ),
        compiler_params=pltpu.CompilerParams(vmem_limit_bytes=40 * 2**20),
        cost_estimate=pl.CostEstimate(
            flops=2 * m * rows * cols,
            bytes_accessed=2 * (feats * rows + rows * cols + m * cols * (2 if with_add else 1)),
            transcendentals=0,
        ),
    )(table, at, b, *args[2:])


def halve(send, keep, n_dp, first):
    stages = n_dp.bit_length() - 1
    for s in range(first, stages):
        got = permute(send, stage_pairs(n_dp, s))
        total = keep.astype(F32) + got.astype(F32)
        if s == stages - 1:
            return total
        total = total.astype(send.dtype)
        edge = total.shape[0] // 2
        keep, send = total[:edge], total[edge:]
    return keep


def scatter_grad(table, at, b, n):
    n_dp = n // 2
    far = grad_half(table, at, b, n, 1)
    got = permute(far, core_pairs(n_dp))
    send, keep = grad_half(table, at, b, n, 0, got)
    return halve(send, keep, n_dp, 0)


def scatter_small(packed, table, n):
    n_dp = n // 2
    placed = jnp.take(packed, table, axis=0)
    edge = n // 2
    near = placed[:edge] + permute(placed[edge:], core_pairs(n_dp))
    return halve(near[edge // 2 :], near[: edge // 2], n_dp, 0)


def col_sum(v):
    return jnp.sum(v.astype(F32), axis=0)


def local(
    n_dp,
    tokens,
    memory,
    token_lengths,
    frame_lengths,
    attention_in,
    attention_out,
    attention_bias,
    norm_gain,
    norm_bias,
    expand_weight,
    expand_bias,
    reduce_weight,
    reduce_bias,
    cotangent,
):
    n = 2 * n_dp
    frame = lax.axis_index("frame")
    me = lax.axis_index("dp") * 2 + frame
    table = jnp.bitwise_xor(me, jnp.asarray(place_table(n_dp))[frame]).astype(jnp.int32)
    nb, rows = tokens.shape[0], tokens.shape[3]
    half = memory.shape[3]
    frames = 2 * half
    total_rows = nb * rows

    own_mem = lax.dynamic_index_in_dim(memory[:, 0], frame, 1, False)
    far_mem = lax.dynamic_index_in_dim(memory[:, 0], 1 - frame, 1, False)
    mem = jnp.concatenate([own_mem, permute(far_mem, core_pairs(n_dp))], axis=1)
    mem = mem.reshape(nb * frames, D)

    tok_len = lax.dynamic_index_in_dim(token_lengths[:, 0], frame, 1, False)
    frm_len = lax.dynamic_index_in_dim(frame_lengths[:, 0], frame, 1, False)
    tok_seg = segment_ids(tok_len, rows)
    frm_seg = segment_ids(frm_len, frames)
    frm_seg = jnp.where(frame == 0, frm_seg, jnp.roll(frm_seg, -half, axis=1))
    pos = jnp.arange(rows, dtype=jnp.int32)
    self_mask = (tok_seg[:, :, None] == tok_seg[:, None, :]) & (pos[None, :] <= pos[:, None])[None]
    cross_mask = tok_seg[:, :, None] == frm_seg[:, None, :]

    def attend(q, k, v, mask):
        s = jnp.einsum(
            "bqhd,bkhd->bhqk", heads(q, nb), heads(k, nb), preferred_element_type=F32
        ) * FACTOR
        s = jnp.where(mask[:, None], s, -1e30)
        e = jnp.exp(s - jnp.max(s, axis=-1, keepdims=True))
        p = (e / jnp.sum(e, axis=-1, keepdims=True)).astype(BF)
        c = jnp.einsum("bhqk,bkhd->bqhd", p, heads(v, nb), preferred_element_type=F32)
        return p, c.reshape(total_rows, D).astype(BF)

    def attend_back(p, q, k, v, dc):
        dch = heads(dc, nb)
        dp = jnp.einsum("bqhd,bkhd->bhqk", dch, heads(v, nb), preferred_element_type=F32)
        pf = p.astype(F32)
        ds = (pf * (dp - jnp.sum(dp * pf, axis=-1, keepdims=True))).astype(BF)
        dq = jnp.einsum("bhqk,bkhd->bqhd", ds, heads(k, nb), preferred_element_type=F32) * FACTOR
        dk = jnp.einsum("bhqk,bqhd->bkhd", ds, heads(q, nb), preferred_element_type=F32) * FACTOR
        dv = jnp.einsum("bhqk,bqhd->bkhd", p, dch, preferred_element_type=F32)
        return [x.reshape(-1, D).astype(BF) for x in (dq, dk, dv)]

    w_in, w_out, bias = attention_in, attention_out, attention_bias
    h = tokens.reshape(total_rows, D).astype(F32)
    n0, r0 = norm_stats(h)
    a0 = (n0 * norm_gain[0] + norm_bias[0]).astype(BF)
    q = (dot(a0, w_in[0, 0]) + bias[0, 0]).astype(BF)
    k = dot(a0, w_in[0, 1]).astype(BF)
    v = (dot(a0, w_in[0, 2]) + bias[0, 1]).astype(BF)
    p, c = attend(q, k, v, self_mask)
    h1 = h + dot(c, w_out[0]) + bias[0, 2]
    n1, r1 = norm_stats(h1)
    a1 = (n1 * norm_gain[1] + norm_bias[1]).astype(BF)
    cq = (dot(a1, w_in[1, 0]) + bias[1, 0]).astype(BF)
    ck = dot(mem, w_in[1, 1]).astype(BF)
    cv = (dot(mem, w_in[1, 2]) + bias[1, 1]).astype(BF)
    cp, cc = attend(cq, ck, cv, cross_mask)
    h2 = h1 + dot(cc, w_out[1]) + bias[1, 2]
    n2, r2 = norm_stats(h2)
    a2 = (n2 * norm_gain[2] + norm_bias[2]).astype(BF)
    u = dot(a2, expand_weight) + expand_bias
    g, pull_act = jax.vjp(lambda x: jax.nn.gelu(x, approximate=True), u)
    g = g.astype(BF)
    h3 = h2 + dot(g, reduce_weight) + reduce_bias
    n3, r3 = norm_stats(h3)
    out = (n3 * norm_gain[3] + norm_bias[3]).astype(BF)
    e3 = cotangent.reshape(total_rows, D).astype(F32)
    dh3 = norm_back(e3, n3, r3, norm_gain[3])
    df = dh3.astype(BF)
    half_cols = D // 2
    gT = g.T
    grad_reduce = [
        scatter_grad(table, gT, df[:, i * half_cols : (i + 1) * half_cols], n) for i in range(2)
    ]
    du = pull_act(dot_t(df, reduce_weight))[0].astype(BF)
    ff = expand_weight.shape[1]
    a2T = a2.T
    grad_expand = [
        scatter_grad(table, a2T, du[:, i * ff // 2 : (i + 1) * ff // 2], n) for i in range(2)
    ]
    e2 = dot_t(du, expand_weight)
    dh2 = dh3 + norm_back(e2, n2, r2, norm_gain[2])
    dx2 = dh2.astype(BF)
    grad_out1 = scatter_grad(table, cc.T, dx2, n)
    dcc = dot_t(dx2, w_out[1]).astype(BF)
    dcq, dck, dcv = attend_back(cp, cq, ck, cv, dcc)
    grad_q1 = scatter_grad(table, a1.T, dcq, n)
    dckv = jnp.concatenate([dck, dcv], axis=1)
    grad_kv1 = scatter_grad(table, mem.T, dckv, n)
    e1 = dot_t(dcq, w_in[1, 0])
    grad_mem = (dot_t(dck, w_in[1, 1]) + dot_t(dcv, w_in[1, 2])).reshape(nb, frames, D)
    own_gm = grad_mem[:, :half]
    far_gm = permute(grad_mem[:, half:], core_pairs(n_dp))
    grad_memory = jnp.where(
        frame == 0, jnp.stack([own_gm, far_gm], axis=1), jnp.stack([far_gm, own_gm], axis=1)
    )[:, None]
    dh1 = dh2 + norm_back(e1, n1, r1, norm_gain[1])
    dx1 = dh1.astype(BF)
    grad_out0 = scatter_grad(table, c.T, dx1, n)
    dc = dot_t(dx1, w_out[0]).astype(BF)
    dq, dk, dv = attend_back(p, q, k, v, dc)
    dqkv = jnp.concatenate([dq, dk, dv], axis=1)
    grad_qkv0 = scatter_grad(table, a0.T, dqkv, n)
    e0 = dot_t(dq, w_in[0, 0]) + dot_t(dk, w_in[0, 1]) + dot_t(dv, w_in[0, 2])
    grad_tokens = dh1 + norm_back(e0, n0, r0, norm_gain[0])

    small = jnp.concatenate(
        [
            x.reshape(n, -1)
            for x in (
                col_sum(dq), col_sum(dv), col_sum(dx1), col_sum(dcq), col_sum(dcv), col_sum(dx2),
                col_sum(e0 * n0), col_sum(e1 * n1), col_sum(e2 * n2), col_sum(e3 * n3),
                col_sum(e0), col_sum(e1), col_sum(e2), col_sum(e3),
                col_sum(du), col_sum(df),
            )
        ],
        axis=1,
    )
    small = scatter_small(small, table, n)[0]
    w = D // n
    grad_bias = small[: 6 * w].reshape(2, 3, w)
    grad_gain = small[6 * w : 10 * w].reshape(4, w)
    grad_shift = small[10 * w : 14 * w].reshape(4, w)
    wide = ff // n
    grad_eb = small[14 * w : 14 * w + wide]
    grad_rb = small[14 * w + wide :]

    kv = jnp.split(grad_kv1, 2, axis=1)
    qkv = jnp.split(grad_qkv0, 3, axis=1)
    grad_in = jnp.stack([jnp.stack(qkv), jnp.stack([grad_q1] + kv)])
    grad_out = jnp.stack([grad_out0, grad_out1])
    shape = tokens.shape
    return (
        out.reshape(shape),
        grad_tokens.reshape(shape),
        grad_memory,
        grad_in,
        grad_out,
        grad_bias,
        grad_gain,
        grad_shift,
        jnp.concatenate(grad_expand, axis=1),
        grad_eb,
        jnp.concatenate(grad_reduce, axis=1),
        grad_rb,
    )


def solution(mesh):
    spread = P(None, "dp", "frame", None, None)
    by_frame = P(None, "dp", None, "frame", None)
    both = ("dp", "frame")
    lengths = P(None, "dp", None, None)
    return jax.shard_map(
        functools.partial(local, mesh.shape["dp"]),
        mesh=mesh,
        in_specs=(spread, by_frame, lengths, lengths) + (P(),) * 9 + (spread,),
        out_specs=(
            spread,
            spread,
            by_frame,
            P(None, None, both, None),
            P(None, both, None),
            P(None, None, both),
            P(None, both),
            P(None, both),
            P(both, None),
            P(both),
            P(both, None),
            P(both),
        ),
        check_vma=False,
    )
```

time: 1500 us -> 574 us (0.38)
  waiting for transfers between devices: 983 us -> 131 us
  matrix products: 240 us -> 136 us
  Pallas kernels: 0 us -> 63.2 us
  other arithmetic: 103 us -> 49.3 us
  starting transfers between devices: 2.15 us -> 52.2 us
  blocking collectives: 48.3 us -> 0 us
  local copies, waits for them, and re-layouts: 97.9 us -> 131 us
    reduce_scatter x6 -> x0, waiting for transfers between devices: 769 us -> none  [the longest x1 253 us: local(): lax.psum_scatter(grad_attention_in, ('dp', 'frame'), scatter_dimension=2,...]
    unnamed x18 -> x0, waiting for transfers between devices: 209 us -> none
    ppermute x0 -> x52, waiting for transfers between devices: none -> 131 us  [permute(): return lax.ppermute(x, AXES, pairs)]
    dot_general x84 -> x30, matrix products: 240 us -> 120 us  [the longest x10 49 us: dot_t(): lax.dot_general(a, b, (((1,), (1,)), ((), ())), preferred_element_type=F32)]
    pallas_call x0 -> x18, Pallas kernels: none -> 63.2 us  [grad_half(): pl.pallas_call(functools.partial(grad_kernel, half, n_half, r, with_add),...]
    ppermute x0 -> x52, starting transfers between devices: none -> 52.2 us  [permute(): return lax.ppermute(x, AXES, pairs)]
    unnamed x1 -> x0, blocking collectives: 40.6 us -> none
    reshape x8 -> x35, local copies, waits for them, and re-layouts: 24.9 us -> 54.1 us  [the longest x16 48.1 us: heads(): return x.reshape(nb, -1, HEADS, HEAD_DIM)]
  transfers between devices with their start and end apart: 15 -> 52, of which waited for: 7 -> 26; matrix products, arithmetic and copies ran while one was open for 20% -> 21% of each run, Pallas kernels for 0% -> 11%
where the time goes in v1:
time: 574 us; the launch traced here: 565 us
  matrix products  136 us (24%)
  local copies, waits for them, and re-layouts  131 us (23%)
  waiting for transfers between devices  131 us (23%)
  Pallas kernels  63.2 us (11%)
  starting transfers between devices  52.2 us (9%)
  other arithmetic  49.3 us (9%)
    ppermute x52, waiting for transfers between devices, permute(): return lax.ppermute(x, AXES, pairs)  131 us
    pallas_call x18, Pallas kernels, grad_half(): pl.pallas_call(functools.partial(grad_kernel, half, n_half, r, with_add),...  63.2 us
    ppermute x52, starting transfers between devices, permute(): return lax.ppermute(x, AXES, pairs)  52.2 us
    dot_general x10, matrix products, dot_t(): lax.dot_general(a, b, (((1,), (1,)), ((), ())), preferred_element_type=F32)  49 us
    reshape x16, local copies, waits for them, and re-layouts, heads(): return x.reshape(nb, -1, HEADS, HEAD_DIM)  48.1 us
    dot_general x10, matrix products, dot(): return jnp.dot(a, b, preferred_element_type=F32)  45.5 us
    unnamed x222, local copies, waits for them, and re-layouts  28.7 us
    convert_element_type x12, local copies, waits for them, and re-layouts, attend_back(): return [x.reshape(-1, D).astype(BF) for x in (dq, dk, dv)]  21.3 us
  transfers between devices with their start and end apart: 52, of which 26 were waited for; matrix products, arithmetic and copies ran while one was open for 21% of the time, Pallas kernels for 11%

profile of v1, /device:TPU:0, one launch (start us, length us, event | category | flops | bytes accessed | tf_op | source)
XLA Modules:
  0.0 564.9 jit_solution(4283976722232704789)
XLA Ops:
  28.1 7.8 %fusion.170 = (f32[2,16,256]{2,1,0:T(8,128)S(1)}, f32[2,16,256,256]{2,3,1,0:T(8,128)}) fusion(pred[2,256,256]{1,2,0:T(8,128)(4,1)S(1)} %get-tuple-element.149, bf16[2,256,16,64]{1,3,2,0:T(8,128)(2,1)} %copy.148, bf16[2,256,16,64]{1,3,2,0:T(8,128)(2,1)} %copy.149), kind=kOutput, calls=%fused_computation.302 | convolution fusion | flops 276824320 | bytes 10649600 | tf_op jit(solution)/shard_map/sub | solution.py:242
  84.0 8.0 %fusion.172 = (f32[2,16,256]{2,1,0:T(8,128)S(1)}, f32[2,16,256,256]{2,3,1,0:T(8,128)}) fusion(pred[2,256,256]{1,2,0:T(8,128)(4,1)S(1)} %get-tuple-element.148, bf16[2,256,16,64]{1,3,2,0:T(8,128)(2,1)} %copy.159, bf16[2,256,16,64]{1,3,2,0:T(8,128)(2,1)} %copy.160), kind=kOutput, calls=%fused_computation.304 | convolution fusion | flops 276824320 | bytes 10649600 | tf_op jit(solution)/shard_map/sub | solution.py:242
  102.8 13.0 %fusion.20 = (bf16[4096,512]{1,0:T(8,128)(2,1)}, f32[512,4096]{0,1:T(8,128)}) fusion(f32[4096]{0:T(1024)S(1)} %copy-done.99, bf16[1024,4096]{1,0:T(8,128)(2,1)} %param.24, f32[512,1024]{1,0:T(8,128)S(1)} %get-tuple-element.159, f32[1024]{0:T(1024)S(1)} %bitcast.375, f32[1024]{0:T(1024)S(1)} %bitcast.365, f32[512]{0:T(512)S(1)} %add_rsqrt_fusion.1, ...), kind=kOutput, calls=%fused_computation.28 | convolution fusion | flops 4318560256 | bytes 23097344 | tf_op jit(solution)/shard_map/dot_general | solution.py:21
  115.9 8.8 %fusion.174 = (f32[512]{0:T(512)S(1)}, f32[512,1024]{1,0:T(8,128)S(1)}) fusion(f32[1024]{0:T(1024)S(1)} %copy-done.100, f32[512,1024]{1,0:T(8,128)S(1)} %get-tuple-element.159, bf16[4096,1024]{1,0:T(8,128)(2,1)S(1)} %bitcast.391, f32[512,4096]{0,1:T(8,128)} %get-tuple-element.176, f32[4096]{0:T(1024)S(1)} %copy-done.99), kind=kOutput, calls=%fused_computation.306 | convolution fusion | flops 4317511168 | bytes 20994048 | tf_op jit(solution)/shard_map/dot_general | solution.py:21
  128.3 12.3 %convert_reduce_fusion = (f32[4096]{0:T(1024)S(1)}, bf16[512,4096]{0,1:T(8,128)(2,1)S(1)}) fusion(f32[512,4096]{0,1:T(8,128)} %get-tuple-element.176, f32[4096]{0:T(1024)S(1)} %copy-done.99, bf16[512,1024]{1,0:T(8,128)(2,1)S(1)} %get-tuple-element.103, bf16[4096,1024]{1,0:T(8,128)(2,1)S(1)} %bitcast.391), kind=kOutput, calls=%fused_computation.29 | convolution fusion | flops 4343197696 | bytes 22052864 | tf_op jit(solution)/shard_map/dot_general | solution.py:25
  142.9 7.1 %fusion.175 = f32[512,1024]{1,0:T(8,128)S(1)} fusion(bf16[512,4096]{0,1:T(8,128)(2,1)S(1)} %get-tuple-element.105, bf16[1024,4096]{1,0:T(8,128)(2,1)} %param.24), kind=kOutput, calls=%fused_computation.307 | convolution fusion | flops 4294967296 | bytes 14680064 | tf_op jit(solution)/shard_map/dot_general | solution.py:25
  165.5 5.0 convert_reduce_fusion.5
  200.9 4.6 fusion.5
  233.4 5.0 fusion.140
  253.0 7.0 %fusion.87 = (f32[1024]{0:T(1024)S(1)}, f32[512]{0:T(512)S(1)}, f32[512]{0:T(512)S(1)}, f32[1024]{0:T(1024)S(1)}, bf16[512,1024]{1,0:T(8,128)(2,1)}, /*index=5*/f32[512,1024]{1,0:T(8,128)}) fusion(bf16[2,1,1,256,1024]{4,3,2,1,0:T(8,128)(2,1)S(1)} %copy-done.43, f32[512]{0:T(512)S(1)} %bitcast.380, f32[512]{0:T(512)S(1)} %bitcast.378, ...), kind=kOutput, calls=%fused_computation.115 | convolution fusion | flops 1081603072 | bytes 11558912 | tf_op jit(solution)/shard_map/dot_general | solution.py:25
  343.4 4.9 collective-permute-done.8
  350.8 6.7 %collective-permute-done.24 = bf16[128,1024]{1,0:T(8,128)(2,1)S(1)} collective-permute-done((bf16[128,1024]{1,0:T(8,128)(2,1)S(1)}, bf16[128,1024]{1,0:T(8,128)(2,1)S(1)}, u32[]{:S(2)}, u32[]{:S(2)}) %collective-permute-start.24) | collective-permute-done | bytes 262176 | tf_op jit(solution)/shard_map/ppermute | solution.py:93
  389.2 5.1 shard_map.238
  420.1 4.9 shard_map.251
  435.7 9.5 %collective-permute-done.33 = bf16[256,2048]{1,0:T(8,128)(2,1)S(1)} collective-permute-done((bf16[256,2048]{1,0:T(8,128)(2,1)S(1)}, bf16[256,2048]{1,0:T(8,128)(2,1)S(1)}, u32[]{:S(2)}, u32[]{:S(2)}) %collective-permute-start.33) | collective-permute-done | bytes 1048608 | tf_op jit(solution)/shard_map/ppermute | solution.py:93
  447.0 9.4 %collective-permute-done.38 = bf16[256,2048]{1,0:T(8,128)(2,1)S(1)} collective-permute-done((bf16[256,2048]{1,0:T(8,128)(2,1)S(1)}, bf16[256,2048]{1,0:T(8,128)(2,1)S(1)}, u32[]{:S(2)}, u32[]{:S(2)}) %collective-permute-start.38) | collective-permute-done | bytes 1048608 | tf_op jit(solution)/shard_map/ppermute | solution.py:93
  459.0 5.9 %shard_map.239 = (bf16[256,3072]{1,0:T(8,128)(2,1)S(1)}, bf16[256,3072]{1,0:T(8,128)(2,1)S(1)}) custom-call(s32[32]{0:T(128)S(1)} %fusion.156.table_ref, bf16[1024,512]{1,0:T(8,128)(2,1)S(1)} %copy-done.28, bf16[512,3072]{1,0:T(8,128)(2,1)S(1)} %pad_maximum_fusion.b_ref, bf16[512,3072]{1,0:T(8,128)(2,1)} %collective-permute-done.2.rest_0_), custom_call_target="tpu_custom_call" | custom-call | flops 1610612736 | bytes 10485760 | tf_op jit(solution)/shard_map/pallas_call | solution.py:145
  474.1 8.4 %collective-permute-done.39 = bf16[128,2048]{1,0:T(8,128)(2,1)S(1)} collective-permute-done((bf16[128,2048]{1,0:T(8,128)(2,1)S(1)}, bf16[128,2048]{1,0:T(8,128)(2,1)S(1)}, u32[]{:S(2)}, u32[]{:S(2)}) %collective-permute-start.39) | collective-permute-done | bytes 524320 | tf_op jit(solution)/shard_map/ppermute | solution.py:93
  485.3 7.5 %collective-permute-done.14 = bf16[128,2048]{1,0:T(8,128)(2,1)S(1)} collective-permute-done((bf16[128,2048]{1,0:T(8,128)(2,1)S(1)}, bf16[128,2048]{1,0:T(8,128)(2,1)S(1)}, u32[]{:S(2)}, u32[]{:S(2)}) %collective-permute-start.14) | collective-permute-done | bytes 524320 | tf_op jit(solution)/shard_map/ppermute | solution.py:93
  503.6 14.6 %collective-permute-done.36 = bf16[32,2048]{1,0:T(8,128)(2,1)S(1)} collective-permute-done((bf16[32,2048]{1,0:T(8,128)(2,1)S(1)}, bf16[32,2048]{1,0:T(8,128)(2,1)S(1)}, u32[]{:S(2)}, u32[]{:S(2)}) %collective-permute-start.36) | collective-permute-done | bytes 131104 | tf_op jit(solution)/shard_map/ppermute | solution.py:93
  518.3 7.1 %collective-permute-done.16 = bf16[32,2048]{1,0:T(8,128)(2,1)S(1)} collective-permute-done((bf16[32,2048]{1,0:T(8,128)(2,1)S(1)}, bf16[32,2048]{1,0:T(8,128)(2,1)S(1)}, u32[]{:S(2)}, u32[]{:S(2)}) %collective-permute-start.16) | collective-permute-done | bytes 131104 | tf_op jit(solution)/shard_map/ppermute | solution.py:93
  526.3 19.0 %collective-permute-done.4 = bf16[128,3072]{1,0:T(8,128)(2,1)S(1)} collective-permute-done((bf16[128,3072]{1,0:T(8,128)(2,1)S(1)}, bf16[128,3072]{1,0:T(8,128)(2,1)S(1)}, u32[]{:S(2)}, u32[]{:S(2)}) %collective-permute-start.4) | collective-permute-done | bytes 786464 | tf_op jit(solution)/shard_map/ppermute | solution.py:93
  547.4 6.0 %collective-permute-done.5 = bf16[64,3072]{1,0:T(8,128)(2,1)S(1)} collective-permute-done((bf16[64,3072]{1,0:T(8,128)(2,1)S(1)}, bf16[64,3072]{1,0:T(8,128)(2,1)S(1)}, u32[]{:S(2)}, u32[]{:S(2)}) %collective-permute-start.5) | collective-permute-done | bytes 393248 | tf_op jit(solution)/shard_map/ppermute | solution.py:93
  555.0 8.4 %collective-permute-done.6 = bf16[32,3072]{1,0:T(8,128)(2,1)S(1)} collective-permute-done((bf16[32,3072]{1,0:T(8,128)(2,1)S(1)}, bf16[32,3072]{1,0:T(8,128)(2,1)S(1)}, u32[]{:S(2)}, u32[]{:S(2)}) %collective-permute-start.6) | collective-permute-done | bytes 196640 | tf_op jit(solution)/shard_map/ppermute | solution.py:93
  (553 shorter events, 365.5 us)
Async XLA Ops:
  3.0 57.1 %collective-permute-start = (bf16[2,128,1024]{2,1,0:T(8,128)(2,1)}, bf16[2,128,1024]{2,1,0:T(8,128)(2,1)}, u32[]{:S(2)}, u32[]{:S(2)}) collective-permute-start(bf16[2,128,1024]{2,1,0:T(8,128)(2,1)} %get-tuple-element.123), channel_id=1, source_target_pairs={{0,1},{1,0},{2,3},{3,2},{4,5},{5,4},{6,7},{7,6},{8,9},{9,8},{10,11... | collective-permute-start | bytes 1572872 | tf_op jit(solution)/shard_map/ppermute | solution.py:93
  241.6 154.4 %collective-permute-start.42 = (bf16[2048,512]{1,0:T(8,128)(2,1)}, bf16[2048,512]{1,0:T(8,128)(2,1)}, u32[]{:S(2)}, u32[]{:S(2)}) collective-permute-start(bf16[2048,512]{1,0:T(8,128)(2,1)} %shard_map.252), channel_id=1, source_target_pairs={{0,1},{1,0},{2,3},{3,2},{4,5},{5,4},{6,7},{7,6},{8,9},{9,8},{10,11... | collective-permute-start | bytes 6291464 | tf_op jit(solution)/shard_map/ppermute | solution.py:93
  261.9 47.7 %collective-permute-start.27 = (f32[16,608]{1,0:T(8,128)S(1)}, f32[16,608]{1,0:T(8,128)S(1)}, u32[]{:S(2)}, u32[]{:S(2)}) collective-permute-start(f32[16,608]{1,0:T(8,128)S(1)} %slice.458), channel_id=1, source_target_pairs={{0,1},{1,0},{2,3},{3,2},{4,5},{5,4},{6,7},{7,6},{8,9},{9,8},{10,11... | collective-permute-start | bytes 116744 | tf_op jit(solution)/shard_map/ppermute | solution.py:93
  264.8 56.1 %collective-permute-start.17 = (bf16[512,1024]{1,0:T(8,128)(2,1)}, bf16[512,1024]{1,0:T(8,128)(2,1)}, u32[]{:S(2)}, u32[]{:S(2)}) collective-permute-start(bf16[512,1024]{1,0:T(8,128)(2,1)} %shard_map.244), channel_id=1, source_target_pairs={{0,1},{1,0},{2,3},{3,2},{4,5},{5,4},{6,7},{7,6},{8,9},{9,8},{10,11... | collective-permute-start | bytes 3145736 | tf_op jit(solution)/shard_map/ppermute | solution.py:93
  267.3 61.8 %collective-permute-start.22 = (bf16[512,1024]{1,0:T(8,128)(2,1)}, bf16[512,1024]{1,0:T(8,128)(2,1)}, u32[]{:S(2)}, u32[]{:S(2)}) collective-permute-start(bf16[512,1024]{1,0:T(8,128)(2,1)} %shard_map.246), channel_id=1, source_target_pairs={{0,1},{1,0},{2,3},{3,2},{4,5},{5,4},{6,7},{7,6},{8,9},{9,8},{10,11... | collective-permute-start | bytes 3145736 | tf_op jit(solution)/shard_map/ppermute | solution.py:93
  271.7 62.5 %collective-permute-start.7 = (bf16[512,1024]{1,0:T(8,128)(2,1)}, bf16[512,1024]{1,0:T(8,128)(2,1)}, u32[]{:S(2)}, u32[]{:S(2)}) collective-permute-start(bf16[512,1024]{1,0:T(8,128)(2,1)} %shard_map.240), channel_id=1, source_target_pairs={{0,1},{1,0},{2,3},{3,2},{4,5},{5,4},{6,7},{7,6},{8,9},{9,8},{10,11... | collective-permute-start | bytes 3145736 | tf_op jit(solution)/shard_map/ppermute | solution.py:93
  320.9 87.0 %collective-permute-start.47 = (bf16[2048,512]{1,0:T(8,128)(2,1)}, bf16[2048,512]{1,0:T(8,128)(2,1)}, u32[]{:S(2)}, u32[]{:S(2)}) collective-permute-start(bf16[2048,512]{1,0:T(8,128)(2,1)} %copy-done.33), channel_id=1, source_target_pairs={{0,1},{1,0},{2,3},{3,2},{4,5},{5,4},{6,7},{7,6},{8,9},{9,8},{10,11... | collective-permute-start | bytes 6291464 | tf_op jit(solution)/shard_map/ppermute | solution.py:93
  334.3 29.0 %collective-permute-start.1 = (f32[2,128,1024]{2,1,0:T(8,128)S(1)}, f32[2,128,1024]{2,1,0:T(8,128)S(1)}, u32[]{:S(2)}, u32[]{:S(2)}) collective-permute-start(f32[2,128,1024]{2,1,0:T(8,128)S(1)} %copy-done.72), channel_id=1, source_target_pairs={{0,1},{1,0},{2,3},{3,2},{4,5},{5,4},{6,7},{7,6},{8,9},{9,8},{10,11... | collective-permute-start | bytes 3145736 | tf_op jit(solution)/shard_map/ppermute | solution.py:93
  363.2 49.5 %collective-permute-start.32 = (bf16[512,2048]{1,0:T(8,128)(2,1)}, bf16[512,2048]{1,0:T(8,128)(2,1)}, u32[]{:S(2)}, u32[]{:S(2)}) collective-permute-start(bf16[512,2048]{1,0:T(8,128)(2,1)} %shard_map.248), channel_id=1, source_target_pairs={{0,1},{1,0},{2,3},{3,2},{4,5},{5,4},{6,7},{7,6},{8,9},{9,8},{10,11... | collective-permute-start | bytes 6291464 | tf_op jit(solution)/shard_map/ppermute | solution.py:93
  368.3 49.9 %collective-permute-start.37 = (bf16[512,2048]{1,0:T(8,128)(2,1)}, bf16[512,2048]{1,0:T(8,128)(2,1)}, u32[]{:S(2)}, u32[]{:S(2)}) collective-permute-start(bf16[512,2048]{1,0:T(8,128)(2,1)} %shard_map.250), channel_id=1, source_target_pairs={{0,1},{1,0},{2,3},{3,2},{4,5},{5,4},{6,7},{7,6},{8,9},{9,8},{10,11... | collective-permute-start | bytes 6291464 | tf_op jit(solution)/shard_map/ppermute | solution.py:93
  389.2 35.8 %collective-permute-start.12 = (bf16[512,2048]{1,0:T(8,128)(2,1)}, bf16[512,2048]{1,0:T(8,128)(2,1)}, u32[]{:S(2)}, u32[]{:S(2)}) collective-permute-start(bf16[512,2048]{1,0:T(8,128)(2,1)} %shard_map.242), channel_id=1, source_target_pairs={{0,1},{1,0},{2,3},{3,2},{4,5},{5,4},{6,7},{7,6},{8,9},{9,8},{10,11... | collective-permute-start | bytes 6291464 | tf_op jit(solution)/shard_map/ppermute | solution.py:93
  396.0 62.2 %collective-permute-start.2 = (bf16[512,3072]{1,0:T(8,128)(2,1)}, bf16[512,3072]{1,0:T(8,128)(2,1)}, u32[]{:S(2)}, u32[]{:S(2)}) collective-permute-start(bf16[512,3072]{1,0:T(8,128)(2,1)} %shard_map.238), channel_id=1, source_target_pairs={{0,1},{1,0},{2,3},{3,2},{4,5},{5,4},{6,7},{7,6},{8,9},{9,8},{10,11... | collective-permute-start | bytes 9437192 | tf_op jit(solution)/shard_map/ppermute | solution.py:93
  418.3 27.0 %collective-permute-start.33 = (bf16[256,2048]{1,0:T(8,128)(2,1)S(1)}, bf16[256,2048]{1,0:T(8,128)(2,1)S(1)}, u32[]{:S(2)}, u32[]{:S(2)}) collective-permute-start(bf16[256,2048]{1,0:T(8,128)(2,1)S(1)} %get-tuple-element.41), channel_id=1, source_target_pairs={{0,2},{1,5},{2,0},{3,7},{4,6},{5,1},{6,4},{7,3},{8,10},{9,13},{10,... | collective-permute-start | bytes 3145736 | tf_op jit(solution)/shard_map/ppermute | solution.py:93
  425.0 31.5 %collective-permute-start.38 = (bf16[256,2048]{1,0:T(8,128)(2,1)S(1)}, bf16[256,2048]{1,0:T(8,128)(2,1)S(1)}, u32[]{:S(2)}, u32[]{:S(2)}) collective-permute-start(bf16[256,2048]{1,0:T(8,128)(2,1)S(1)} %get-tuple-element.43), channel_id=1, source_target_pairs={{0,2},{1,5},{2,0},{3,7},{4,6},{5,1},{6,4},{7,3},{8,10},{9,13},{10,... | collective-permute-start | bytes 3145736 | tf_op jit(solution)/shard_map/ppermute | solution.py:93
  430.4 37.3 %collective-permute-start.13 = (bf16[256,2048]{1,0:T(8,128)(2,1)S(1)}, bf16[256,2048]{1,0:T(8,128)(2,1)S(1)}, u32[]{:S(2)}, u32[]{:S(2)}) collective-permute-start(bf16[256,2048]{1,0:T(8,128)(2,1)S(1)} %get-tuple-element.35), channel_id=1, source_target_pairs={{0,2},{1,5},{2,0},{3,7},{4,6},{5,1},{6,4},{7,3},{8,10},{9,13},{10,... | collective-permute-start | bytes 3145736 | tf_op jit(solution)/shard_map/ppermute | solution.py:93
  434.0 35.1 %collective-permute-start.44 = (bf16[512,512]{1,0:T(8,128)(2,1)S(1)}, bf16[512,512]{1,0:T(8,128)(2,1)S(1)}, u32[]{:S(2)}, u32[]{:S(2)}) collective-permute-start(bf16[512,512]{1,0:T(8,128)(2,1)S(1)} %slice.487), channel_id=1, source_target_pairs={{0,8},{1,9},{2,10},{3,11},{4,12},{5,13},{6,14},{7,15},{8,0},{9,1},... | collective-permute-start | bytes 1572872 | tf_op jit(solution)/shard_map/ppermute | solution.py:93
  445.2 25.6 %collective-permute-start.49 = (bf16[512,512]{1,0:T(8,128)(2,1)S(1)}, bf16[512,512]{1,0:T(8,128)(2,1)S(1)}, u32[]{:S(2)}, u32[]{:S(2)}) collective-permute-start(bf16[512,512]{1,0:T(8,128)(2,1)S(1)} %slice.494), channel_id=1, source_target_pairs={{0,8},{1,9},{2,10},{3,11},{4,12},{5,13},{6,14},{7,15},{8,0},{9,1},... | collective-permute-start | bytes 1572872 | tf_op jit(solution)/shard_map/ppermute | solution.py:93
  458.3 24.2 %collective-permute-start.39 = (bf16[128,2048]{1,0:T(8,128)(2,1)S(1)}, bf16[128,2048]{1,0:T(8,128)(2,1)S(1)}, u32[]{:S(2)}, u32[]{:S(2)}) collective-permute-start(bf16[128,2048]{1,0:T(8,128)(2,1)S(1)} %slice.479), channel_id=1, source_target_pairs={{0,8},{1,9},{2,10},{3,11},{4,12},{5,13},{6,14},{7,15},{8,0},{9,1},... | collective-permute-start | bytes 1572872 | tf_op jit(solution)/shard_map/ppermute | solution.py:93
  467.7 57.7 %collective-permute-start.3 = (bf16[256,3072]{1,0:T(8,128)(2,1)S(1)}, bf16[256,3072]{1,0:T(8,128)(2,1)S(1)}, u32[]{:S(2)}, u32[]{:S(2)}) collective-permute-start(bf16[256,3072]{1,0:T(8,128)(2,1)S(1)} %get-tuple-element.31), channel_id=1, source_target_pairs={{0,2},{1,5},{2,0},{3,7},{4,6},{5,1},{6,4},{7,3},{8,10},{9,13},{10,... | collective-permute-start | bytes 4718600 | tf_op jit(solution)/shard_map/ppermute | solution.py:93
  469.1 23.6 %collective-permute-start.14 = (bf16[128,2048]{1,0:T(8,128)(2,1)S(1)}, bf16[128,2048]{1,0:T(8,128)(2,1)S(1)}, u32[]{:S(2)}, u32[]{:S(2)}) collective-permute-start(bf16[128,2048]{1,0:T(8,128)(2,1)S(1)} %slice.440), channel_id=1, source_target_pairs={{0,8},{1,9},{2,10},{3,11},{4,12},{5,13},{6,14},{7,15},{8,0},{9,1},... | collective-permute-start | bytes 1572872 | tf_op jit(solution)/shard_map/ppermute | solution.py:93
  470.9 23.8 %collective-permute-start.45 = (bf16[256,512]{1,0:T(8,128)(2,1)S(1)}, bf16[256,512]{1,0:T(8,128)(2,1)S(1)}, u32[]{:S(2)}, u32[]{:S(2)}) collective-permute-start(bf16[256,512]{1,0:T(8,128)(2,1)S(1)} %slice.489), channel_id=1, source_target_pairs={{0,4},{1,3},{2,6},{3,1},{4,0},{5,7},{6,2},{7,5},{8,12},{9,11},{10,... | collective-permute-start | bytes 786440 | tf_op jit(solution)/shard_map/ppermute | solution.py:93
  495.1 23.1 %collective-permute-start.46 = (bf16[128,512]{1,0:T(8,128)(2,1)S(1)}, bf16[128,512]{1,0:T(8,128)(2,1)S(1)}, u32[]{:S(2)}, u32[]{:S(2)}) collective-permute-start(bf16[128,512]{1,0:T(8,128)(2,1)S(1)} %slice.491), channel_id=1, source_target_pairs={{0,16},{1,17},{2,18},{3,19},{4,20},{5,21},{6,22},{7,23},{8,24},{9,... | collective-permute-start | bytes 393224 | tf_op jit(solution)/shard_map/ppermute | solution.py:93
  496.8 29.3 %collective-permute-start.51 = (bf16[128,512]{1,0:T(8,128)(2,1)S(1)}, bf16[128,512]{1,0:T(8,128)(2,1)S(1)}, u32[]{:S(2)}, u32[]{:S(2)}) collective-permute-start(bf16[128,512]{1,0:T(8,128)(2,1)S(1)} %slice.498), channel_id=1, source_target_pairs={{0,16},{1,17},{2,18},{3,19},{4,20},{5,21},{6,22},{7,23},{8,24},{9,... | collective-permute-start | bytes 393224 | tf_op jit(solution)/shard_map/ppermute | solution.py:93
  501.9 24.3 %collective-permute-start.41 = (bf16[32,2048]{1,0:T(8,128)(2,1)S(1)}, bf16[32,2048]{1,0:T(8,128)(2,1)S(1)}, u32[]{:S(2)}, u32[]{:S(2)}) collective-permute-start(bf16[32,2048]{1,0:T(8,128)(2,1)S(1)} %slice.483), channel_id=1, source_target_pairs={{0,16},{1,17},{2,18},{3,19},{4,20},{5,21},{6,22},{7,23},{8,24},{9,... | collective-permute-start | bytes 393224 | tf_op jit(solution)/shard_map/ppermute | solution.py:93
  (133 other events, 1193.8 us)
